TPU v7x, 256 devices: a whole 4x4x8 slice. The times are simulated.
256 devices in a mesh: dp: 4 (over y), seq: 64 (over x, z, core).
Axes of the slice: x: 4, y: 4, z: 8, core: 2. Of those that a mesh axis runs over, the one named last changes fastest.
Arguments:
- hidden_in: bfloat16 [65536, 2048], P(('dp', 'seq')), parts along dimension 0, may hold values from -6 to 6
- lin_query: bfloat16 [65536, 1024], P(('dp', 'seq')), parts along dimension 0, may hold values from -6 to 6
- lin_key: bfloat16 [65536, 256], P(('dp', 'seq')), parts along dimension 0, may hold values from -6 to 6
- lin_value: bfloat16 [65536, 256], P(('dp', 'seq')), parts along dimension 0, may hold values from -6 to 6
- lin_gain: float32 [1024], replicated, may hold values from 0.1 to 1.9
- lin_out_weight: bfloat16 [1024, 2048], replicated, may hold values from -0.1875 to 0.1875
- soft_gain: float32 [2048], replicated, may hold values from 0.1 to 1.9
- soft_wq: bfloat16 [2048, 1024], replicated, may hold values from -4 to 4
- soft_wk: bfloat16 [2048, 256], replicated, may hold values from -4 to 4
- soft_wv: bfloat16 [2048, 256], replicated, may hold values from -0.125 to 0.125
- pattern: int32 [2, 128, 18], replicated, may hold values from 0 to 127, as said below
Outputs:
- attended: bfloat16 [65536, 1024], P(('dp', 'seq')), parts along dimension 0
There are 4 independent parts, one for each index of `dp`. A program takes and returns all parts, laid end to end along the dimension named above; an argument that names none is the same for every part. Nothing has to cross between parts.
Inputs may be any that keep to these rules, and one draw needn't show every extreme that they name: pattern[g, b, 0] = b and pattern[g, b, 1] = max(b - 1, 0); every entry of row b lies between 0 and b; for each key-value head and the 2 query blocks held by one device, the entries in slots 2 to 17 of those rows that lie in another device's tokens all name the same key block of that device.
All inputs are finite; a program needn't handle non-finite values.
Results may differ from a plain program's by a relative error of at most 0.035.
Values may be sent and summed in bfloat16 or wider, within the bound.
A program may use at most 128 MiB of HBM per device.

v0:
```python
import jax
import jax.numpy as jnp
from jax import lax
from jax.sharding import PartitionSpec as P

HEAD_DIM = 128
HEADS = 8
KV_HEADS = 2
BLOCK = 128
EPSILON = 1e-06


def carried_in(shard, axis, combine, identity):
    devices, position = (lax.axis_size(axis), lax.axis_index(axis))
    everything = lax.all_gather(shard, axis)
    start = jnp.broadcast_to(jnp.asarray(identity, shard.dtype), shard.shape)

    def lap(k, before):
        reached = k < position
        new = combine(before, everything[k])
        return jnp.where(reached, new, before)

    return lax.fori_loop(0, devices, lap, start)


def add_states(earlier, later):
    return earlier + later


def local(
    hidden_in,
    lin_query,
    lin_key,
    lin_value,
    lin_gain,
    lin_out_weight,
    soft_gain,
    soft_wq,
    soft_wk,
    soft_wv,
    pattern,
):
    tok_count = hidden_in.shape[0]
    local_blocks = tok_count // BLOCK
    per_group = HEADS // KV_HEADS
    listed = pattern.shape[2]
    position = lax.axis_index("seq")
    query_blocks = lin_query.reshape(local_blocks, BLOCK, KV_HEADS, per_group, HEAD_DIM)
    key_blocks = lin_key.reshape(local_blocks, BLOCK, KV_HEADS, HEAD_DIM)
    value_blocks = lin_value.reshape(local_blocks, BLOCK, KV_HEADS, HEAD_DIM)
    block_states = jnp.einsum(
        "ntgd,ntge->ngde", key_blocks, value_blocks, preferred_element_type=jnp.float32
    )
    device_state = jnp.sum(block_states, axis=0)
    carried = carried_in(device_state, "seq", add_states, jnp.zeros_like(device_state))
    running = jnp.concatenate(
        [jnp.zeros_like(block_states[:1]), jnp.cumsum(block_states[:-1], axis=0)], axis=0
    )
    before = carried[None] + running
    inter = jnp.einsum(
        "ntgpd,ngde->ntgpe",
        query_blocks.astype(jnp.float32),
        before,
        precision=lax.Precision.HIGHEST,
    )
    rows_here = jnp.arange(BLOCK)
    causal = rows_here[:, None] >= rows_here[None, :]
    local_scores = jnp.einsum(
        "ntgpd,nsgd->ngpts", query_blocks, key_blocks, preferred_element_type=jnp.float32
    )
    local_scores = jnp.where(causal, local_scores, 0.0).astype(jnp.bfloat16)
    intra = jnp.einsum(
        "ngpts,nsge->ntgpe", local_scores, value_blocks, preferred_element_type=jnp.float32
    )
    mixed = (inter + intra).reshape(tok_count, HEADS, HEAD_DIM)
    normed = (
        mixed
        * lax.rsqrt(jnp.mean(mixed * mixed, axis=-1, keepdims=True) + EPSILON)
        * lin_gain.reshape(HEADS, HEAD_DIM)
    )
    normed = normed.reshape(tok_count, HEADS * HEAD_DIM).astype(jnp.bfloat16)
    branch = jnp.dot(normed, lin_out_weight, preferred_element_type=jnp.float32)
    residual = (hidden_in.astype(jnp.float32) + branch).astype(jnp.bfloat16)
    widened = residual.astype(jnp.float32)
    layer_in = (
        widened
        * lax.rsqrt(jnp.mean(widened * widened, axis=-1, keepdims=True) + EPSILON)
        * soft_gain
    ).astype(jnp.bfloat16)
    soft_query = jnp.dot(layer_in, soft_wq, preferred_element_type=jnp.float32).astype(jnp.bfloat16)
    soft_key = jnp.dot(layer_in, soft_wk, preferred_element_type=jnp.float32).astype(jnp.bfloat16)
    soft_value = jnp.dot(layer_in, soft_wv, preferred_element_type=jnp.float32).astype(jnp.bfloat16)
    packed = jnp.concatenate(
        [
            soft_key.reshape(tok_count, KV_HEADS, HEAD_DIM),
            soft_value.reshape(tok_count, KV_HEADS, HEAD_DIM),
        ],
        axis=-1,
    )
    mine = lax.dynamic_slice_in_dim(pattern, position * local_blocks, local_blocks, 1)
    whole = lax.all_gather(packed, "seq", axis=0, tiled=True)
    table = whole.reshape(-1, BLOCK, KV_HEADS, 2 * HEAD_DIM)
    group_ids = jnp.arange(KV_HEADS)[:, None, None]
    tiles = table[mine, :, group_ids, :]
    tiles = tiles.reshape(KV_HEADS, local_blocks, listed * BLOCK, 2 * HEAD_DIM)
    keys_tile = tiles[..., :HEAD_DIM]
    values_tile = tiles[..., HEAD_DIM:]
    soft_blocks = soft_query.reshape(local_blocks, BLOCK, KV_HEADS, per_group, HEAD_DIM)
    scores = jnp.einsum(
        "ntgpd,gnkd->gnptk", soft_blocks, keys_tile, preferred_element_type=jnp.float32
    ) * HEAD_DIM ** (-0.5)
    same = mine[..., :, None] == mine[..., None, :]
    earlier = jnp.arange(listed)[None, :] < jnp.arange(listed)[:, None]
    repeated = jnp.any(same & earlier, axis=-1)
    live = jnp.repeat(jnp.logical_not(repeated), BLOCK, axis=-1)
    columns = jnp.arange(listed * BLOCK)
    causal_keys = (columns[None, :] >= BLOCK) | (columns[None, :] <= rows_here[:, None])
    allowed = live[:, :, None, None, :] & causal_keys[None, None, None]
    highest = jnp.max(jnp.where(allowed, scores, -jnp.inf), axis=-1, keepdims=True)
    weights = jnp.where(allowed, jnp.exp(scores - highest), 0.0)
    total = jnp.sum(weights, axis=-1, keepdims=True)
    probs = (weights / total).astype(jnp.bfloat16)
    attended = jnp.einsum(
        "gnptk,gnke->ntgpe", probs, values_tile, preferred_element_type=jnp.float32
    )
    return attended.reshape(tok_count, HEADS * HEAD_DIM).astype(jnp.bfloat16)


def solution(mesh):
    in_specs = (
        P(("dp", "seq"), None),
        P(("dp", "seq"), None),
        P(("dp", "seq"), None),
        P(("dp", "seq"), None),
        P(),
        P(),
        P(),
        P(),
        P(),
        P(),
        P(),
    )
    out_specs = P(("dp", "seq"), None)
    return jax.shard_map(local, mesh=mesh, in_specs=in_specs, out_specs=out_specs, check_vma=False)
```

profile of v0, /device:TPU:1, one launch (start us, length us, event | category | flops | bytes accessed | tf_op | source)
XLA Modules:
  0.0 329.4 jit_solution(11226672005344907080)
XLA Ops:
  6.5 1.0 reshape.120
  9.5 1.4 reshape.122
  10.9 86.4 %all-gather.6.cloned.1.call-done = f32[128,128,128]{2,1,0:T(8,128)} async-done(((f32[2,128,128]{2,1,0:T(8,128)}), f32[128,128,128]{2,1,0:T(8,128)}) %all-gather.6.cloned.1.call-update) | async-done | bytes 8388624 | tf_op jit(solution)/shard_map/all_gather | solution.py:15
  97.4 62.3 %while.14 = (s32[]{:T(128)}, f32[2,128,128]{2,1,0:T(8,128)S(1)}, s32[]{:T(128)}, f32[64,2,128,128]{3,2,1,0:T(8,128)}, s32[]{:T(128)}, /*index=5*/s32[]{:T(128)}) while((s32[]{:T(128)}, f32[2,128,128]{2,1,0:T(8,128)S(1)}, s32[]{:T(128)}, f32[64,2,128,128]{3,2,1,0:T(8,128)}, s32[]{:T(128)}, /*index=5*/s32[]{:T(128)}) %tuple.44), condition=%wide.region_2.3_spmd.clone, body=%wide.region_1.2_spmd.clone.sunk | while | flops 98308 | bytes 393317 | solution.py:23
  98.4 0.9 add_select_fusion.2
  99.3 0.9 add_select_fusion.2
  100.3 0.9 add_select_fusion.2
  101.3 0.9 add_select_fusion.2
  102.2 0.9 add_select_fusion.2
  103.2 0.9 add_select_fusion.2
  104.2 0.9 add_select_fusion.2
  105.2 0.9 add_select_fusion.2
  106.1 0.9 add_select_fusion.2
  107.1 0.9 add_select_fusion.2
  108.1 0.9 add_select_fusion.2
  109.1 0.9 add_select_fusion.2
  110.0 0.9 add_select_fusion.2
  111.0 0.9 add_select_fusion.2
  112.0 0.9 add_select_fusion.2
  113.0 0.9 add_select_fusion.2
  113.9 0.9 add_select_fusion.2
  114.9 0.9 add_select_fusion.2
  115.9 0.9 add_select_fusion.2
  116.9 0.9 add_select_fusion.2
  117.8 0.9 add_select_fusion.2
  118.8 0.9 add_select_fusion.2
  119.8 0.9 add_select_fusion.2
  120.7 0.9 add_select_fusion.2
  121.7 0.9 add_select_fusion.2
  122.7 0.9 add_select_fusion.2
  123.7 0.9 add_select_fusion.2
  124.6 0.9 add_select_fusion.2
  125.6 0.9 add_select_fusion.2
  126.6 0.9 add_select_fusion.2
  160.3 1.5 multiply_reduce_fusion
  161.9 1.7 copy.85
  164.4 3.9 %fusion.13 = (f32[256]{0:T(256)S(1)}, bf16[256,2048]{1,0:T(8,128)(2,1)S(1)}) fusion(bf16[1024,2048]{1,0:T(8,128)(2,1)} %param.18, f32[256,1024]{1,0:T(8,128)S(1)} %reshape.123, f32[32,8,8,128]{3,2,1,0:T(8,128)S(1)} %bitcast.81, f32[1024]{0:T(1024)S(1)} %copy-done.4, bf16[256,2048]{1,0:T(8,128)(2,1)} %param.13), kind=kOutput, calls=%fused_computation.24 | convolution fusion | flops 1077673728 | bytes 8393728 | tf_op jit(solution)/shard_map/dot_general | solution.py:82
  169.4 2.2 convolution_convert_fusion.2
  173.3 1.2 fusion.29
  174.5 1.7 broadcast_and_fusion
  176.3 3.8 %convolution_convert_fusion = bf16[256,1024]{1,0:T(8,128)(2,1)S(1)} fusion(bf16[2048,1024]{1,0:T(8,128)(2,1)} %param.20, bf16[256,2048]{1,0:T(8,128)(2,1)} %copy-done.5, f32[2048]{0:T(1024)S(1)} %copy-done.3, f32[256]{0:T(256)S(1)} %add_rsqrt_fusion.1), kind=kOutput, calls=%fused_computation.34 | convolution fusion | flops 1076101120 | bytes 5776384 | tf_op jit(solution)/shard_map/dot_general | solution.py:90
  180.4 89.2 %all-gather.4.cloned.1.call-done = bf16[16384,2,256]{2,0,1:T(8,128)(2,1)} async-done(((bf16[256,2,256]{2,0,1:T(8,128)(2,1)}), bf16[16384,2,256]{2,0,1:T(8,128)(2,1)}) %all-gather.4.cloned.1.call-update) | async-done | bytes 16777232 | tf_op jit(solution)/shard_map/all_gather | solution.py:101
  269.6 14.0 %copy.90 = bf16[128,128,2,256]{3,1,2,0:T(8,128)(2,1)} copy(bf16[128,128,2,256]{3,1,0,2:T(8,128)(2,1)} %bitcast.76) | data formatting | bytes 33554432 | tf_op jit(solution)/shard_map/reshape | solution.py:102
  283.6 12.9 %gather_fusion = bf16[72,128,256]{2,1,0:T(8,128)(2,1)} fusion(bf16[128,128,2,256]{3,1,2,0:T(8,128)(2,1)} %copy.90, s32[72]{0:T(128)S(1)} %reshape.129), kind=kCustom, calls=%fused_computation | custom fusion | bytes 9437760 | tf_op jit(solution)/shard_map/gather | solution.py:104
  296.5 4.3 %fusion.11 = f32[2,2,2304,128,4]{3,2,4,1,0:T(8,128)S(1)} fusion(bf16[2,2,2304,256]{3,2,1,0:T(8,128)(2,1)} %bitcast.77, bf16[2,128,2,4,128]{4,3,2,1,0:T(4,128)(2,1)S(1)} %reshape.128), kind=kOutput, calls=%fused_computation.20 | convolution fusion | flops 1207959552 | bytes 21757952 | tf_op jit(solution)/shard_map/ntgpd,gnkd->gnptk/dot_general | solution.py:109
  300.8 11.6 %fusion.64 = (f32[2,2,4,128]{3,2,1,0:T(4,128)S(1)}, f32[2,2,4,128,2304]{3,4,2,1,0:T(8,128)}) fusion(f32[2,2,2304,128,4]{3,2,4,1,0:T(8,128)S(1)} %fusion.11, pred[2,2,128,2304]{2,3,1,0:T(8,128)(4,1)S(1)} %broadcast_and_fusion), kind=kOutput, calls=%fused_computation.76 | output fusion | flops 28313856 | bytes 38936576 | tf_op jit(solution)/shard_map/sub | solution.py:120
  312.3 8.8 %fusion.24 = bf16[2,128,2,4,128]{1,4,3,2,0:T(8,128)(2,1)S(1)} fusion(f32[2,2,4,128,2304]{3,4,2,1,0:T(8,128)} %get-tuple-element.117, f32[2,2,4,128]{3,2,1,0:T(4,128)S(1)} %get-tuple-element.116, bf16[2,2,2304,256]{3,2,1,0:T(8,128)(2,1)} %bitcast.78), kind=kOutput, calls=%fused_computation.35 | convolution fusion | flops 1217658880 | bytes 21766144 | tf_op jit(solution)/shard_map/gnptk,gnke->ntgpe/dot_general | solution.py:123
  321.4 1.2 convert_element_type.52
  (78 shorter events, 39.1 us)
Async XLA Ops:
  6.5 161.8 %copy-start = (bf16[2048,256]{1,0:T(8,128)(2,1)S(1)}, bf16[2048,256]{1,0:T(8,128)(2,1)}, u32[]{:S(2)}) copy-start(bf16[2048,256]{1,0:T(8,128)(2,1)} %param.22) | copy-start | bytes 3145732
  6.5 90.8 %all-gather.6.cloned.1.call-start = ((), (), s32[]{:S(2)}) async-start(), calls=%async_computation.1 | async-start | bytes 8519680 | tf_op jit(solution)/shard_map/all_gather | solution.py:15
  9.4 260.2 %all-gather.4.cloned.1.call-start = ((), (), s32[]{:S(2)}) async-start(), calls=%async_computation | async-start | bytes 17039360 | tf_op jit(solution)/shard_map/all_gather | solution.py:101
  159.7 4.7 %copy-start.4 = (f32[1024]{0:T(1024)S(1)}, f32[1024]{0:T(1024)}, u32[]{:S(2)}) copy-start(f32[1024]{0:T(1024)} %param.17) | copy-start | bytes 12292
  164.4 4.0 %copy-start.3 = (f32[2048]{0:T(1024)S(1)}, f32[2048]{0:T(1024)}, u32[]{:S(2)}) copy-start(f32[2048]{0:T(1024)} %param.19) | copy-start | bytes 24580
  168.3 1.0 copy-start.5
  168.3 4.2 %copy-start.2 = (s32[2,128,18]{1,0,2:T(2,128)S(1)}, s32[2,128,18]{1,0,2:T(2,128)}, u32[]{:S(2)}) copy-start(s32[2,128,18]{1,0,2:T(2,128)} %param.23) | copy-start | bytes 55300
  312.3 10.3 %copy-start.1 = (bf16[2048,256]{1,0:T(8,128)(2,1)S(1)}, bf16[2048,256]{1,0:T(8,128)(2,1)}, u32[]{:S(2)}) copy-start(bf16[2048,256]{1,0:T(8,128)(2,1)} %param.22) | copy-start | bytes 3145732
Sparse Core Ops, SparseCore 0:
  10.1 87.1 all-gather.5
  172.6 96.9 all-gather.3
where the time goes:
time: 331 us; the launch traced here: 329 us
  waiting for transfers between devices  176 us (53%)
  other arithmetic  76.4 us (23%)
  local copies, waits for them, and re-layouts  35.5 us (11%)
  matrix products  26.7 us (8%)
  between operations  13.7 us (4%)
    all_gather x1, waiting for transfers between devices, local(): whole = lax.all_gather(packed, 'seq', axis=0, tiled=True)  89.2 us
    all_gather x1, waiting for transfers between devices, carried_in(): everything = lax.all_gather(shard, axis)  86.4 us
    select_n x64, other arithmetic, lap(): return jnp.where(reached, new, before)  60.8 us
    reshape x1, local copies, waits for them, and re-layouts, local(): table = whole.reshape(-1, BLOCK, KV_HEADS, 2 * HEAD_DIM)  14 us
    gather x1, local copies, waits for them, and re-layouts, local(): tiles = table[mine, :, group_ids, :]  12.9 us
    sub x1, other arithmetic, local(): weights = jnp.where(allowed, jnp.exp(scores - highest), 0.0)  11.6 us
    dot_general x1, matrix products, local(): jnp.einsum('gnptk,gnke->ntgpe', probs, values_tile, preferred_element_typ...  8.79 us
  transfers between devices with their start and end apart: 2, of which 2 were waited for; matrix products, arithmetic and copies ran while one was open for 3% of the time, Pallas kernels for 0%

commit v1 on v0

--- a/solution.py
+++ b/solution.py
@@ -98,7 +98,8 @@
         axis=-1,
     )
     mine = lax.dynamic_slice_in_dim(pattern, position * local_blocks, local_blocks, 1)
-    whole = lax.all_gather(packed, "seq", axis=0, tiled=True)
+    sent = jnp.stack([packed] * lax.axis_size("seq"))
+    whole = jnp.concatenate(lax.all_to_all(sent, "seq", 0, 0), axis=0)
     table = whole.reshape(-1, BLOCK, KV_HEADS, 2 * HEAD_DIM)
     group_ids = jnp.arange(KV_HEADS)[:, None, None]
     tiles = table[mine, :, group_ids, :]

time: 331 us -> 611 us (1.85)
  waiting for transfers between devices: 176 us -> 444 us
  local copies, waits for them, and re-layouts: 35.5 us -> 42.3 us
  starting transfers between devices: 0.04 us -> 6.57 us
    all_to_all x0 -> x1, waiting for transfers between devices: none -> 358 us  [local(): whole = jnp.concatenate(lax.all_to_all(sent, 'seq', 0, 0), axis=0)]
    all_gather x1 -> x0, waiting for transfers between devices: 89.2 us -> none  [local(): whole = lax.all_gather(packed, 'seq', axis=0, tiled=True)]
    reshape x3 -> x0, local copies, waits for them, and re-layouts: 14.2 us -> none  [the longest x1 14 us: local(): table = whole.reshape(-1, BLOCK, KV_HEADS, 2 * HEAD_DIM)]
    another operation x0 -> x2, local copies, waits for them, and re-layouts: none -> 12.6 us  [the longest x1 6.58 us: local(): table = whole.reshape(-1, BLOCK, KV_HEADS, 2 * HEAD_DIM)]
    all_to_all x0 -> x1, local copies, waits for them, and re-layouts: none -> 8.6 us  [local(): whole = jnp.concatenate(lax.all_to_all(sent, 'seq', 0, 0), axis=0)]
    all_to_all x0 -> x1, starting transfers between devices: none -> 6.57 us  [local(): whole = jnp.concatenate(lax.all_to_all(sent, 'seq', 0, 0), axis=0)]
  transfers between devices with their start and end apart: 2 -> 2, of which waited for: 2 -> 2; matrix products, arithmetic and copies ran while one was open for 3% -> 2% of each run, Pallas kernels for 0% -> 0%
where the time goes in v1:
time: 611 us; the launch traced here: 609 us
  waiting for transfers between devices  444 us (73%)
  other arithmetic  75.8 us (12%)
  local copies, waits for them, and re-layouts  42.3 us (7%)
  matrix products  25.2 us (4%)
  between operations  13.7 us (2%)
  starting transfers between devices  6.57 us (1%)
    all_to_all x1, waiting for transfers between devices, local(): whole = jnp.concatenate(lax.all_to_all(sent, 'seq', 0, 0), axis=0)  358 us
    all_gather x1, waiting for transfers between devices, carried_in(): everything = lax.all_gather(shard, axis)  86.5 us
    select_n x64, other arithmetic, lap(): return jnp.where(reached, new, before)  60.9 us
    gather x1, local copies, waits for them, and re-layouts, local(): tiles = table[mine, :, group_ids, :]  12.8 us
  transfers between devices with their start and end apart: 2, of which 2 were waited for; matrix products, arithmetic and copies ran while one was open for 2% of the time, Pallas kernels for 0%

profile of v1, /device:TPU:1, one launch (start us, length us, event | category | flops | bytes accessed | tf_op | source)
XLA Modules:
  0.0 609.2 jit_solution(4661039865929463582)
XLA Ops:
  6.5 1.0 reshape.119
  9.5 1.4 reshape.121
  10.9 86.5 %all-gather.3.cloned.1.call-done = f32[128,128,128]{2,1,0:T(8,128)} async-done(((f32[2,128,128]{2,1,0:T(8,128)}), f32[128,128,128]{2,1,0:T(8,128)}) %all-gather.3.cloned.1.call-update) | async-done | bytes 8388624 | tf_op jit(solution)/shard_map/all_gather | solution.py:15
  97.4 62.4 %while.14 = (s32[]{:T(128)}, f32[2,128,128]{2,1,0:T(8,128)S(1)}, s32[]{:T(128)}, f32[64,2,128,128]{3,2,1,0:T(8,128)}, s32[]{:T(128)}, /*index=5*/s32[]{:T(128)}) while((s32[]{:T(128)}, f32[2,128,128]{2,1,0:T(8,128)S(1)}, s32[]{:T(128)}, f32[64,2,128,128]{3,2,1,0:T(8,128)}, s32[]{:T(128)}, /*index=5*/s32[]{:T(128)}) %tuple.42), condition=%wide.region_2.3_spmd.clone, body=%wide.region_1.2_spmd.clone.sunk | while | flops 98308 | bytes 393317 | solution.py:23
  98.4 1.0 add_select_fusion.2
  99.3 1.0 add_select_fusion.2
  100.3 1.0 add_select_fusion.2
  101.3 1.0 add_select_fusion.2
  102.3 1.0 add_select_fusion.2
  103.2 1.0 add_select_fusion.2
  104.2 1.0 add_select_fusion.2
  105.2 1.0 add_select_fusion.2
  106.2 1.0 add_select_fusion.2
  107.1 1.0 add_select_fusion.2
  108.1 1.0 add_select_fusion.2
  109.1 1.0 add_select_fusion.2
  110.1 1.0 add_select_fusion.2
  111.0 1.0 add_select_fusion.2
  112.0 1.0 add_select_fusion.2
  113.0 1.0 add_select_fusion.2
  114.0 1.0 add_select_fusion.2
  114.9 1.0 add_select_fusion.2
  125.7 1.0 add_select_fusion.2
  127.6 1.0 add_select_fusion.2
  129.6 1.0 add_select_fusion.2
  131.5 1.0 add_select_fusion.2
  133.5 1.0 add_select_fusion.2
  144.2 1.0 add_select_fusion.2
  146.2 1.0 add_select_fusion.2
  148.1 1.0 add_select_fusion.2
  150.1 1.0 add_select_fusion.2
  152.0 1.0 add_select_fusion.2
  160.4 1.5 multiply_reduce_fusion
  162.1 1.7 copy.86
  164.5 4.0 fusion.13
  170.1 6.1 stack.2
  176.2 6.6 %all-to-all-start = ((bf16[64,256,2,256]{3,1,2,0:T(8,128)(2,1)}), bf16[64,256,2,256]{3,1,2,0:T(8,128)(2,1)}, u32[]{:S(2)}, u32[]{:S(2)}) async-start(bf16[64,256,2,256]{3,1,2,0:T(8,128)(2,1)} %stack.2), calls=%async_computation | async-start | bytes 33554432 | tf_op jit(solution)/shard_map/all_to_all | solution.py:102
  183.6 1.2 fusion.29
  184.8 1.7 broadcast_and_fusion
  186.5 3.8 convolution_convert_fusion
  190.7 357.6 %all-to-all-done = bf16[64,256,2,256]{3,1,2,0:T(8,128)(2,1)} async-done(((bf16[64,256,2,256]{3,1,2,0:T(8,128)(2,1)}), bf16[64,256,2,256]{3,1,2,0:T(8,128)(2,1)}, u32[]{:S(2)}, u32[]{:S(2)}) %all-to-all-start) | async-done | bytes 16777248 | tf_op jit(solution)/shard_map/all_to_all | solution.py:102
  548.3 8.6 %copy.89 = bf16[64,256,2,256]{3,1,0,2:T(8,128)(2,1)S(1)} copy(bf16[64,256,2,256]{3,1,2,0:T(8,128)(2,1)} %all-to-all-done) | data formatting | bytes 33554432 | tf_op jit(solution)/shard_map/all_to_all | solution.py:102
  556.9 6.6 %copy.91 = bf16[128,128,2,256]{3,1,2,0:T(8,128)(2,1)} copy(bf16[128,128,2,256]{3,1,0,2:T(8,128)(2,1)S(1)} %bitcast.76) | data formatting | bytes 33554432 | tf_op jit(solution)/shard_map/reshape;reshape | solution.py:103
  563.5 12.8 %gather_fusion = bf16[72,128,256]{2,1,0:T(8,128)(2,1)} fusion(bf16[128,128,2,256]{3,1,2,0:T(8,128)(2,1)} %copy.91, s32[72]{0:T(128)S(1)} %reshape.127), kind=kCustom, calls=%fused_computation | custom fusion | bytes 9437760 | tf_op jit(solution)/shard_map/gather | solution.py:105
  576.3 4.3 fusion.11
  580.5 11.5 %fusion.64 = (f32[2,2,4,128]{3,2,1,0:T(4,128)S(1)}, f32[2,2,4,128,2304]{3,4,2,1,0:T(8,128)}) fusion(f32[2,2,2304,128,4]{3,2,4,1,0:T(8,128)S(1)} %fusion.11, pred[2,2,128,2304]{2,3,1,0:T(8,128)(4,1)S(1)} %broadcast_and_fusion), kind=kOutput, calls=%fused_computation.76 | output fusion | flops 28313856 | bytes 38936576 | tf_op jit(solution)/shard_map/sub | solution.py:121
  592.1 8.8 %fusion.24 = bf16[2,128,2,4,128]{1,4,3,2,0:T(8,128)(2,1)S(1)} fusion(f32[2,2,4,128,2304]{3,4,2,1,0:T(8,128)} %get-tuple-element.117, f32[2,2,4,128]{3,2,1,0:T(4,128)S(1)} %get-tuple-element.116, bf16[2,2,2304,256]{3,2,1,0:T(8,128)(2,1)} %bitcast.78), kind=kOutput, calls=%fused_computation.35 | convolution fusion | flops 1217658880 | bytes 21766144 | tf_op jit(solution)/shard_map/gnptk,gnke->ntgpe/dot_general | solution.py:124
  601.2 1.2 convert_element_type.52
  (80 shorter events, 40.6 us)
Async XLA Ops:
  6.5 162.0 %copy-start = (bf16[2048,256]{1,0:T(8,128)(2,1)S(1)}, bf16[2048,256]{1,0:T(8,128)(2,1)}, u32[]{:S(2)}) copy-start(bf16[2048,256]{1,0:T(8,128)(2,1)} %param.22) | copy-start | bytes 3145732
  6.5 90.8 %all-gather.3.cloned.1.call-start = ((), (), s32[]{:S(2)}) async-start(), calls=%async_computation.1 | async-start | bytes 8519680 | tf_op jit(solution)/shard_map/all_gather | solution.py:15
  159.8 4.7 copy-start.5
  164.5 4.1 copy-start.4
  164.5 4.7 copy-start.3
  168.5 1.4 copy-start.6
  176.2 6.6 %copy-start.2 = (s32[2,128,18]{1,0,2:T(2,128)S(1)}, s32[2,128,18]{1,0,2:T(2,128)}, u32[]{:S(2)}) copy-start(s32[2,128,18]{1,0,2:T(2,128)} %param.23) | copy-start | bytes 55300
  176.2 372.1 %all-to-all-start = ((bf16[64,256,2,256]{3,1,2,0:T(8,128)(2,1)}), bf16[64,256,2,256]{3,1,2,0:T(8,128)(2,1)}, u32[]{:S(2)}, u32[]{:S(2)}) async-start(bf16[64,256,2,256]{3,1,2,0:T(8,128)(2,1)} %stack.2), calls=%async_computation | async-start | bytes 33554432 | tf_op jit(solution)/shard_map/all_to_all | solution.py:102
  592.1 10.3 %copy-start.1 = (bf16[2048,256]{1,0:T(8,128)(2,1)S(1)}, bf16[2048,256]{1,0:T(8,128)(2,1)}, u32[]{:S(2)}) copy-start(bf16[2048,256]{1,0:T(8,128)(2,1)} %param.22) | copy-start | bytes 3145732
Sparse Core Ops, SparseCore 0:
  10.1 87.1 all-gather.2
